TPU v7x, 32 devices: a whole 2x2x4 slice. The times are simulated.
32 devices in a mesh: grp: 2 (over y), role: 2 (over core), ctx: 8 (over z, x).
Axes of the slice: x: 2, y: 2, z: 4, core: 2. Of those that a mesh axis runs over, the one named last changes fastest.
Arguments:
- teacher_streams: bfloat16 [3, 8192, 4096], P(None, ('grp', 'ctx'), 'role'), parts along dimension 1, may hold values from -6 to 6
- conv_filter: bfloat16 [4096, 128], P('role'), may hold values from -0.5 to 0.5
- map_weight: bfloat16 [4096, 2048], P(('role', 'ctx')), may hold values from -0.125 to 0.125
- bases: int32 [8192], P(('grp', 'ctx')), parts along dimension 0, may hold values from 0 to 3
- base_weights: float32 [4], replicated, may hold values from 0.25 to 2
- student_qkv: bfloat16 [3, 8192, 2048], P(None, ('grp', 'ctx'), 'role'), parts along dimension 1, may hold values from -6 to 6
Outputs:
- student_grads: bfloat16 [3, 8192, 2048], P(None, ('grp', 'ctx'), 'role'), parts along dimension 1
There are 2 independent parts, one for each index of `grp`. A program takes and returns all parts, laid end to end along the dimension named above; an argument that names none is the same for every part. Nothing has to cross between parts.
All inputs are finite; a program needn't handle non-finite values.
Results may differ from a plain program's by a relative error of at most 0.0055.
Values may be sent and summed in bfloat16 or wider, within the bound.
A program may use at most 192 MiB of HBM per device.

v0:
```python
from functools import reduce

import jax
import jax.numpy as jnp
from jax import lax
from jax.sharding import PartitionSpec as P

DH = 128
BLK = 512


def from_behind(value, axis, steps):
    count = lax.axis_size(axis)
    leading, last = (max(0, -steps), min(count, count - steps))
    return lax.ppermute(value, axis, [(source, source + steps) for source in range(leading, last)])


def prefix(value, axis, join, neutral, backward):
    count, mine = (lax.axis_size(axis), lax.axis_index(axis))
    pieces = lax.all_gather(value, axis)
    if backward:
        pieces = pieces[::-1]
        mine = count - 1 - mine
    so_far = jnp.full_like(value, 0) + jnp.asarray(neutral, value.dtype)

    def turn(position, so_far):
        longer = join(so_far, pieces[position])
        return jnp.where(position < mine, longer, so_far)

    return lax.fori_loop(0, count - 1, turn, so_far)


def depthwise(extended, filters):
    kernel = jnp.flip(filters, axis=1).T[:, None, :]
    result = lax.conv_general_dilated(
        extended[None],
        kernel,
        (1,),
        "VALID",
        dimension_numbers=("NWC", "WIO", "NWC"),
        feature_group_count=extended.shape[1],
        preferred_element_type=jnp.float32,
    )
    return result[0]


def add_states(earlier, later):
    return earlier + later


def on_device(teacher_streams, conv_filter, map_weight, bases, base_weights, student_qkv):
    gate_in = teacher_streams[0]
    mixed_in = (
        teacher_streams[1].astype(jnp.float32) * teacher_streams[2].astype(jnp.float32)
    ).astype(jnp.bfloat16)
    tok_rows = mixed_in.shape[0]
    rim_rows = conv_filter.shape[1] - 1
    left_rim = from_behind(mixed_in[tok_rows - rim_rows :], "ctx", 1)
    conv_out = depthwise(jnp.concatenate([left_rim, mixed_in], 0), conv_filter)
    teacher_out = (gate_in.astype(jnp.float32) * conv_out).astype(jnp.bfloat16)
    zero_map = jnp.zeros((tok_rows, map_weight.shape[1]), jnp.float32)
    shard_rows = lax.all_gather(map_weight, "ctx", axis=0, tiled=True)
    columns = lax.slice_in_dim(teacher_out, 0, shard_rows.shape[0], axis=1)
    partial_map = zero_map + jnp.dot(columns, shard_rows, preferred_element_type=jnp.float32)
    target = lax.psum_scatter(partial_map, "role", scatter_dimension=1, tiled=True)
    head_width = student_qkv.shape[2]
    heads_dev = head_width // DH
    queries = student_qkv[0].reshape(tok_rows, heads_dev, DH)
    keys_all = student_qkv[1].reshape(tok_rows, heads_dev, DH)
    values_all = student_qkv[2].reshape(tok_rows, heads_dev, DH)
    att_scale = float(DH * tok_rows * lax.axis_size("ctx")) ** (-0.5)
    nblocks = tok_rows // BLK
    causal = (jnp.arange(BLK)[:, None] >= jnp.arange(BLK)[None, :])[None]
    state_terms = [
        jnp.einsum("shd,she->hde", keys_all, values_all, preferred_element_type=jnp.float32)
    ]
    zero_state = jnp.zeros((heads_dev, DH, DH), jnp.float32)
    own_state = reduce(jnp.add, state_terms)
    carried = prefix(own_state, "ctx", add_states, zero_state, False)
    outputs = []
    block = 0
    prefix_bf = carried.astype(jnp.bfloat16)
    scores = jnp.einsum("thd,shd->hts", queries, keys_all, preferred_element_type=jnp.float32)
    scores_bf = jnp.where(causal, scores, 0.0).astype(jnp.bfloat16)
    block_out = att_scale * (
        jnp.einsum("thd,hde->the", queries, prefix_bf, preferred_element_type=jnp.float32)
        + jnp.einsum("hts,she->the", scores_bf, values_all, preferred_element_type=jnp.float32)
    )
    prefixes = [prefix_bf]
    kept_scores = [scores_bf]
    outputs.append(block_out.reshape(BLK, head_width))
    outputs = outputs[0]
    onehot = (bases[:, None] == jnp.arange(base_weights.shape[0])[None, :]).astype(jnp.float32)
    tok_weight = jnp.sum(onehot * base_weights[None, :], axis=1)
    resid_bf = (
        (tok_weight[:, None] * (outputs - target))
        .astype(jnp.bfloat16)
        .reshape(tok_rows, heads_dev, DH)
    )
    back_terms = [jnp.einsum("thd,the->hde", queries, resid_bf, preferred_element_type=jnp.float32)]
    own_back = reduce(jnp.add, back_terms)
    later_sum = prefix(own_back, "ctx", add_states, zero_state, True)
    grad_blocks = [None] * nblocks
    for block in reversed(range(nblocks)):
        later_bf = later_sum.astype(jnp.bfloat16)
        later_sum = later_sum + back_terms[block]
        scores_bf = kept_scores[block]
        grad_scores = jnp.where(
            causal,
            jnp.einsum("the,she->hts", resid_bf, values_all, preferred_element_type=jnp.float32),
            0.0,
        ).astype(jnp.bfloat16)
        grad_query = att_scale * (
            jnp.einsum(
                "the,hde->thd", resid_bf, prefixes[block], preferred_element_type=jnp.float32
            )
            + jnp.einsum("hts,shd->thd", grad_scores, keys_all, preferred_element_type=jnp.float32)
        )
        grad_key = att_scale * (
            jnp.einsum("she,hde->shd", values_all, later_bf, preferred_element_type=jnp.float32)
            + jnp.einsum("hts,thd->shd", grad_scores, queries, preferred_element_type=jnp.float32)
        )
        grad_value = att_scale * (
            jnp.einsum("shd,hde->she", keys_all, later_bf, preferred_element_type=jnp.float32)
            + jnp.einsum("hts,the->she", scores_bf, resid_bf, preferred_element_type=jnp.float32)
        )
        grad_blocks[block] = jnp.stack(
            [
                grad_query.reshape(BLK, head_width),
                grad_key.reshape(BLK, head_width),
                grad_value.reshape(BLK, head_width),
            ],
            0,
        ).astype(jnp.bfloat16)
    return grad_blocks[0]


def solution(mesh):
    in_specs = (
        P(None, ("grp", "ctx"), "role"),
        P("role", None),
        P(("role", "ctx"), None),
        P(("grp", "ctx")),
        P(),
        P(None, ("grp", "ctx"), "role"),
    )
    out_specs = P(None, ("grp", "ctx"), "role")
    return jax.shard_map(
        on_device, mesh=mesh, in_specs=in_specs, out_specs=out_specs, check_vma=False
    )
```

profile of v0, /device:TPU:0, one launch (start us, length us, event | category | flops | bytes accessed | tf_op | source)
XLA Modules:
  0.0 349.2 jit_solution(2665267496531229638)
XLA Ops:
  7.3 3.2 multiply_convert_fusion
  11.5 5.6 %collective-permute-start = (bf16[127,2048]{1,0:T(8,128)(2,1)}, bf16[127,2048]{1,0:T(8,128)(2,1)}, u32[]{:S(2)}, u32[]{:S(2)}) collective-permute-start(bf16[127,2048]{1,0:T(8,128)(2,1)} %slice_bitcast_fusion), channel_id=1, source_target_pairs={{0,1},{1,2},{2,3},{3,4},{4,5},{5,6},{6,7},{8,9},{9,10},{10,11},{11... | collective-permute-start | bytes 1560584 | tf_op jit(solution)/shard_map/ppermute | solution.py:15
  17.1 1.3 fusion.17
  21.0 1.5 rev.7
  23.4 3.0 fusion.42
  26.5 8.9 %collective-permute-done = bf16[127,2048]{1,0:T(8,128)(2,1)} collective-permute-done((bf16[127,2048]{1,0:T(8,128)(2,1)}, bf16[127,2048]{1,0:T(8,128)(2,1)}, u32[]{:S(2)}, u32[]{:S(2)}) %collective-permute-start) | collective-permute-done | bytes 520224 | tf_op jit(solution)/shard_map/ppermute | solution.py:15
  35.4 1.7 maximum_bitcast_fusion
  37.1 65.3 %fusion = bf16[1,512,2048]{2,0,1:T(2,128)(2,1)} fusion(bf16[128,1,2048]{2,1,0:T(2,128)(2,1)S(1)} %copy.85, bf16[1,639,2048]{2,1,0:T(8,128)(2,1)S(1)} %maximum_bitcast_fusion, bf16[1,512,2048]{2,1,0:T(8,128)(2,1)S(1)} %slice-done), kind=kOutput, calls=%fused_computation.5 | convolution fusion | flops 271581184 | bytes 7335936 | tf_op jit(solution)/shard_map/conv_general_dilated | solution.py:35
  102.4 40.9 %all-gather.6.cloned.1.call-done = bf16[2048,2048]{1,0:T(8,128)(2,1)} async-done(((bf16[256,2048]{1,0:T(8,128)(2,1)}), bf16[2048,2048]{1,0:T(8,128)(2,1)}) %all-gather.6.cloned.1.call-update) | async-done | bytes 8388624 | tf_op jit(solution)/shard_map/all_gather | solution.py:62
  143.2 11.5 %fusion.2 = f32[512,2048]{1,0:T(8,128)} fusion(bf16[2048,2048]{1,0:T(8,128)(2,1)} %all-gather.6.cloned.1.call-done, bf16[1,512,2048]{2,0,1:T(2,128)(2,1)} %fusion), kind=kOutput, calls=%fused_computation.11 | convolution fusion | flops 4294967296 | bytes 14680064 | tf_op jit(solution)/shard_map/dot_general | solution.py:64
  155.0 1.6 copy.113
  156.8 3.3 select_convert_fusion.1
  160.1 56.9 %all-gather.8.cloned.1.call-done = f32[64,128,128]{2,1,0:T(8,128)} async-done(((f32[8,128,128]{2,1,0:T(8,128)}), f32[64,128,128]{2,1,0:T(8,128)}) %all-gather.8.cloned.1.call-update) | async-done | bytes 4194320 | tf_op jit(solution)/shard_map/all_gather | solution.py:20
  217.0 8.8 %while.28 = (s32[]{:T(128)}, f32[8,128,128]{2,1,0:T(8,128)S(1)}, s32[]{:T(128)}, f32[8,8,128,128]{3,2,1,0:T(8,128)}, s32[]{:T(128)}, /*index=5*/s32[]{:T(128)}) while((s32[]{:T(128)}, f32[8,128,128]{2,1,0:T(8,128)S(1)}, s32[]{:T(128)}, f32[8,8,128,128]{3,2,1,0:T(8,128)}, s32[]{:T(128)}, /*index=5*/s32[]{:T(128)}) %tuple.75), condition=%wide.region_1.2_spmd.clone, body=%wide.region_0.1_spmd.clone.sunk | while | flops 393220 | bytes 1572965 | solution.py:30
  227.3 5.2 %fusion.9 = f32[512,8,128]{0,2,1:T(8,128)} fusion(f32[8,128,512]{2,1,0:T(8,128)S(1)} %fusion.15, bf16[8,512,512]{2,1,0:T(8,128)(2,1)} %select_convert_fusion.1, bf16[512,8,128]{0,2,1:T(8,128)(2,1)S(1)} %bitcast.79), kind=kOutput, calls=%fused_computation.21 | convolution fusion | flops 537919488 | bytes 9437184 | tf_op jit(solution)/shard_map/hts,she->the/dot_general | solution.py:87
  232.5 3.0 copy.86
  235.5 3.5 multiply_convert_fusion.2
  239.0 1.5 copy.114
  240.5 1.6 convolution_bitcast_fusion
  243.6 1.4 select_convert_fusion
  245.0 2.5 fusion.8
  247.5 2.3 copy.97
  249.7 4.4 %fusion.19 = f32[8,128,512]{2,1,0:T(8,128)} fusion(bf16[512,8,128]{0,2,1:T(8,128)(2,1)S(1)} %bitcast.85, bf16[8,512,512]{2,1,0:T(8,128)(2,1)} %select_convert_fusion.1), kind=kOutput, calls=%fused_computation.38 | convolution fusion | flops 536870912 | bytes 7340032 | tf_op jit(solution)/shard_map/hts,the->she/dot_general | solution.py:125
  254.2 61.3 %all-gather.10.cloned.1.call-done = f32[64,128,128]{2,1,0:T(8,128)} async-done(((f32[8,128,128]{2,1,0:T(8,128)}), f32[64,128,128]{2,1,0:T(8,128)}) %all-gather.10.cloned.1.call-update) | async-done | bytes 4194320 | tf_op jit(solution)/shard_map/all_gather | solution.py:20
  315.5 4.6 %rev.8 = f32[8,8,128,128]{3,2,1,0:T(8,128)} reverse(f32[8,8,128,128]{3,2,1,0:T(8,128)} %bitcast.95), dimensions={0} | reverse | bytes 8388608 | tf_op jit(solution)/shard_map/rev | solution.py:22
  320.1 8.7 %while.29 = (s32[]{:T(128)}, f32[8,128,128]{2,1,0:T(8,128)S(1)}, s32[]{:T(128)}, f32[8,8,128,128]{3,2,1,0:T(8,128)}, s32[]{:T(128)}, /*index=5*/s32[]{:T(128)}) while((s32[]{:T(128)}, f32[8,128,128]{2,1,0:T(8,128)S(1)}, s32[]{:T(128)}, f32[8,8,128,128]{3,2,1,0:T(8,128)}, s32[]{:T(128)}, /*index=5*/s32[]{:T(128)}) %tuple.64), condition=%wide.region_5.6_spmd.clone, body=%wide.region_4.5_spmd.clone.sunk | while | flops 393220 | bytes 1572965 | solution.py:30
  328.9 1.8 fusion.11
  331.5 1.5 multiply_convert_fusion.1
  333.0 1.5 copy.99
  334.5 4.7 %fusion.6 = bf16[512,8,128]{0,2,1:T(8,128)(2,1)} fusion(f32[8,128,512]{2,1,0:T(8,128)} %fusion.11, bf16[512,8,128]{0,2,1:T(8,128)(2,1)S(1)} %bitcast.89, bf16[8,512,512]{2,1,0:T(8,128)(2,1)} %copy-done.2), kind=kOutput, calls=%fused_computation.16 | convolution fusion | flops 538443776 | bytes 8388608 | tf_op jit(solution)/shard_map/hts,thd->shd/dot_general | solution.py:121
  339.2 1.5 copy.98
  340.7 2.0 pad_maximum_fusion
  (67 shorter events, 26.8 us)
Async XLA Ops:
  6.5 136.7 %all-gather.6.cloned.1.call-start = ((), (), s32[]{:S(2)}) async-start(), calls=%async_computation.1 | async-start | bytes 9437184 | tf_op jit(solution)/shard_map/all_gather | solution.py:62
  7.3 209.7 %all-gather.8.cloned.1.call-start = ((), (), s32[]{:S(2)}) async-start(), calls=%async_computation.3 | async-start | bytes 4718592 | tf_op jit(solution)/shard_map/all_gather | solution.py:20
  7.3 9.8 %copy-start.11 = (bf16[3,512,1024]{2,1,0:T(8,128)(2,1)S(1)}, bf16[3,512,1024]{2,1,0:T(8,128)(2,1)}, u32[]{:S(2)}) copy-start(bf16[3,512,1024]{2,1,0:T(8,128)(2,1)} %param.15) | copy-start | bytes 9437188
  11.5 23.9 %collective-permute-start = (bf16[127,2048]{1,0:T(8,128)(2,1)}, bf16[127,2048]{1,0:T(8,128)(2,1)}, u32[]{:S(2)}, u32[]{:S(2)}) collective-permute-start(bf16[127,2048]{1,0:T(8,128)(2,1)} %slice_bitcast_fusion), channel_id=1, source_target_pairs={{0,1},{1,2},{2,3},{3,4},{4,5},{5,6},{6,7},{8,9},{9,10},{10,11},{11... | collective-permute-start | bytes 1560584 | tf_op jit(solution)/shard_map/ppermute | solution.py:15
  18.9 1.9 copy-start
  19.5 1.3 copy-start.5
  19.5 1.5 copy-start.12
  20.8 214.7 %reduce-scatter.2.cloned.1.call-start = ((), (), s32[]{:S(2)}) async-start(), calls=%async_computation.2 | async-start | bytes 6291456 | tf_op jit(solution)/shard_map/reduce_scatter | solution.py:65
  26.4 10.7 %slice-start = ((bf16[3,512,2048]{2,1,0:T(8,128)(2,1)}), bf16[1,512,2048]{2,1,0:T(8,128)(2,1)S(1)}, s32[]{:S(2)}) async-start(bf16[3,512,2048]{2,1,0:T(8,128)(2,1)} %param.10), calls=%async_computation.5 | async-start | bytes 4194304 | tf_op jit(solution)/shard_map/slice | solution.py:52
  154.7 1.8 copy-start.13
  154.7 1.9 copy-start.14
  154.7 2.0 copy-start.6
  154.8 160.7 %all-gather.10.cloned.1.call-start = ((), (), s32[]{:S(2)}) async-start(), calls=%async_computation.4 | async-start | bytes 4718592 | tf_op jit(solution)/shard_map/all_gather | solution.py:20
  156.6 69.2 %copy-start.3 = (bf16[1,512,1024]{1,2,0:T(8,128)(2,1)}, bf16[1,512,1024]{1,2,0:T(8,128)(2,1)S(1)}, u32[]{:S(2)}) copy-start(bf16[1,512,1024]{1,2,0:T(8,128)(2,1)S(1)} %copy.113) | copy-start | bytes 3145732
  225.7 1.5 copy-start.1
  243.6 1.4 copy-start.7
  245.0 2.5 copy-start.2
  328.9 1.8 copy-start.8
  328.9 2.7 copy-start.9
  331.5 3.0 copy-start.4
  334.5 6.2 %copy-start.10 = (bf16[1,512,1024]{2,1,0:T(8,128)(2,1)S(1)}, bf16[1,512,1024]{2,1,0:T(8,128)(2,1)}, u32[]{:S(2)}) copy-start(bf16[1,512,1024]{2,1,0:T(8,128)(2,1)} %copy.97) | copy-start | bytes 3145732
Sparse Core Ops, SparseCore 0:
  9.5 133.6 all-gather.5
  145.3 71.5 all-gather.7
  219.2 10.2 reduce-scatter.1
  243.3 72.1 all-gather.9
where the time goes:
time: 350 us; the launch traced here: 349 us
  waiting for transfers between devices  169 us (48%)
  matrix products  105 us (30%)
  other arithmetic  30.7 us (9%)
  local copies, waits for them, and re-layouts  24.8 us (7%)
  between operations  13.5 us (4%)
  starting transfers between devices  5.94 us (2%)
    all_gather x2, waiting for transfers between devices, prefix(): pieces = lax.all_gather(value, axis)  118 us
    conv_general_dilated x1, matrix products, depthwise(): lax.conv_general_dilated(extended[None], kernel, (1,), 'VALID', dimension...  65.3 us
    all_gather x1, waiting for transfers between devices, on_device(): shard_rows = lax.all_gather(map_weight, 'ctx', axis=0, tiled=True)  40.9 us
    select_n x14, other arithmetic, turn(): return jnp.where(position < mine, longer, so_far)  17.2 us
    dot_general x1, matrix products, on_device(): jnp.dot(columns, shard_rows, preferred_element_type=jnp.float32)  11.5 us
    ppermute x1, waiting for transfers between devices, from_behind(): lax.ppermute(value, axis, [(source, source + steps) for source in range(l...  8.95 us
  transfers between devices with their start and end apart: 5, of which 4 were waited for; matrix products, arithmetic and copies ran while one was open for 36% of the time, Pallas kernels for 0%

commit v1 on v0

v1 whole, which is shorter than its diff:
```python
import functools

import jax
import jax.numpy as jnp
import ml_dtypes
import numpy as np
from jax import lax
from jax.experimental import pallas as pl
from jax.experimental.pallas import tpu as pltpu
from jax.sharding import PartitionSpec as P

DH = 128
LANE = 128
BF = jnp.bfloat16
F32 = jnp.float32
MESH = pl.DeviceIdType.MESH


def transform(taps):
    freq = np.arange(taps)[:, None]
    time = np.arange(2 * taps)[None, :]
    angle = np.pi * ((2 * freq + 1) * time % (4 * taps)) / (2 * taps)
    full = np.concatenate([np.cos(angle), -np.sin(angle)], 0)
    back = full[:, taps:].T / taps
    pieces = []
    for matrix in (full, back):
        high = matrix.astype(ml_dtypes.bfloat16)
        low = (matrix - high.astype(np.float64)).astype(ml_dtypes.bfloat16)
        pieces += [high, low]
    return pieces


def dot(a, b, dims=((1,), (0,))):
    return lax.dot_general(a, b, (dims, ((), ())), preferred_element_type=F32)


NT = ((1,), (1,))
TN = ((0,), (0,))


def kernel(
    n, nx, scale,
    streams, filt, wmap, tokw, qkv, fhi, flo, ghi, glo,
    grads,
    wcw, wccw, wy, xbuf, tbuf, tcw, tccw, ty, out, resid, own, exc, prefix, hsend, hrecv, bsend, brecv,
    in_loc, in_send, in_recv, cw_send, cw_recv, cc_send, cc_recv, y_send, y_recv,
    halo_send, halo_recv, t_send, t_recv, h_ssem, h_rsem, b_ssem, b_rsem,
):
    toks, chans = streams.shape[1], streams.shape[2]
    width = qkv.shape[2]
    heads = width // DH
    rows = wmap.shape[0]
    taps = filt.shape[1]
    rounds = hsend.shape[0]
    quarter = width // 4
    cwn = tcw.shape[1]
    common = width // 2
    g, r, me = lax.axis_index("grp"), lax.axis_index("role"), lax.axis_index("ctx")
    nz = n // nx

    def ctx_of(pos):
        pos = lax.rem(pos + n, n)
        x, t = lax.div(pos, nz), lax.rem(pos, nz)
        z = t + lax.rem(x, 2) * (nz - 1 - 2 * t)
        return z * nx + x

    z0, x0 = lax.div(me, nx), lax.rem(me, nx)
    pos = x0 * nz + z0 + lax.rem(x0, 2) * (nz - 1 - 2 * z0)
    nxt, prv = ctx_of(pos + 1), ctx_of(pos - 1)

    bar = pltpu.get_barrier_semaphore()
    for peer in ({"ctx": nxt}, {"ctx": prv}, {"grp": 1 - g}, {"role": 1 - r}):
        pl.semaphore_signal(bar, inc=1, device_id=peer, device_id_type=MESH)
    for k in range(rounds):
        d = 1 << k

        @pl.when(me + d < n)
        def _():
            pl.semaphore_signal(bar, inc=1, device_id={"ctx": me + d}, device_id_type=MESH)

        @pl.when(me >= d)
        def _():
            pl.semaphore_signal(bar, inc=1, device_id={"ctx": me - d}, device_id_type=MESH)

    peers = 4
    for k in range(rounds):
        d = 1 << k
        peers = peers + jnp.where(me + d < n, 1, 0) + jnp.where(me >= d, 1, 0)
    pl.semaphore_wait(bar, peers)

    def span(ctx):
        return pl.ds(pl.multiple_of(ctx * rows, 16), rows)

    def remote(src, dst, ssem, rsem, peer):
        return pltpu.make_async_remote_copy(
            src_ref=src, dst_ref=dst, send_sem=ssem, recv_sem=rsem, device_id=peer, device_id_type=MESH
        )

    def shares(role):
        base = role * width
        mine = base + g * quarter
        other = base + (1 - g) * quarter
        cols = lambda at, size: pl.ds(pl.multiple_of(at, LANE), size)
        return [
            (wmap.at[:, cols(base + common, cwn)], wcw.at[r, span(me), :]),
            (wmap.at[:, cols(base + common + cwn, LANE)], wccw.at[r, span(me), pl.ds(0, LANE)]),
            (wmap.at[:, cols(mine, quarter)], wccw.at[r, span(me), pl.ds(LANE, quarter)]),
            (wmap.at[:, cols(other, quarter)], wy.at[r, span(me), :]),
        ]

    first = [
        remote(src, dst, in_send.at[i], in_recv.at[i], {"role": 1 - r})
        for i, (src, dst) in enumerate(shares(1 - r))
    ]
    for copy in first:
        copy.start()
    local = [
        pltpu.make_async_copy(src, dst, in_loc.at[i]) for i, (src, dst) in enumerate(shares(r))
    ]
    for copy in local:
        copy.start()

    def cw_copy(s):
        at = span(ctx_of(pos - s))
        return remote(wcw.at[:, at, :], wcw.at[:, at, :], cw_send.at[s], cw_recv.at[s], {"ctx": nxt})

    def cw_in(s):
        at = span(ctx_of(pos - s))
        return remote(wcw.at[:, at, :], wcw.at[:, at, :], cw_send.at[s - 1], cw_recv.at[s - 1], {"ctx": nxt})

    def cc_copy(s):
        at = span(ctx_of(pos + s))
        return remote(wccw.at[:, at, :], wccw.at[:, at, :], cc_send.at[s], cc_recv.at[s], {"ctx": prv})

    def cc_in(s):
        at = span(ctx_of(pos + s))
        return remote(wccw.at[:, at, :], wccw.at[:, at, :], cc_send.at[s - 1], cc_recv.at[s - 1], {"ctx": prv})

    def y_copy(s):
        at = span(ctx_of(pos + s))
        return remote(
            wccw.at[:, at, pl.ds(LANE, quarter)], wy.at[:, at, :], y_send.at[s], y_recv.at[s], {"grp": 1 - g}
        )

    def ring_in(s):
        cw_in(s).wait_recv()
        cc_in(s).wait_recv()

        def onward():
            cw_copy(s).start()
            cc_copy(s).start()

        if isinstance(s, int):
            if s < n - 1:
                onward()
        else:
            pl.when(s < n - 1)(onward)
        y_copy(s).start()

    def mix():
        @pl.loop(0, toks // 128)
        def _(b):
            at = pl.ds(pl.multiple_of(b * 128, 128), 128)
            xbuf[pl.ds(pl.multiple_of(b * 128 + taps, 128), 128), :] = (
                streams[1, at, :].astype(F32) * streams[2, at, :].astype(F32)
            ).astype(BF)

    halo = remote(
        xbuf.at[pl.ds(toks, taps), :], xbuf.at[pl.ds(0, taps), :], halo_send, halo_recv, {"ctx": me + 1}
    )

    def head(h):
        return pl.ds(pl.multiple_of(h * DH, DH), DH)

    def scan_send(k, up, send, recv, ssem, rsem):
        d = 1 << k
        send[k] = (own[...] + exc[...]).astype(BF)

        @pl.when((me + d < n) if up else (me >= d))
        def _():
            scan_copy(k, up, send, recv, ssem, rsem).start()

    def scan_copy(k, up, send, recv, ssem, rsem):
        d = 1 << k
        return remote(send.at[k], recv.at[k], ssem.at[k], rsem.at[k], {"ctx": me + d if up else me - d})

    def scan_recv(k, up, send, recv, ssem, rsem):
        d = 1 << k

        @pl.when((me >= d) if up else (me + d < n))
        def _():
            scan_copy(k, up, send, recv, ssem, rsem).wait_recv()
            exc[...] += recv[k].astype(F32)

    def scan_done(k, up, send, recv, ssem, rsem):
        d = 1 << k

        @pl.when((me + d < n) if up else (me >= d))
        def _():
            scan_copy(k, up, send, recv, ssem, rsem).wait_send()

    fwd = (True, hsend, hrecv, h_ssem, h_rsem)
    bwd = (False, bsend, brecv, b_ssem, b_rsem)

    def own_state():
        exc[...] = jnp.zeros_like(exc)

        @pl.loop(0, heads)
        def _(h):
            own[h] = dot(qkv[1, :, head(h)], qkv[2, :, head(h)], TN)

    tile = 256

    def conv(blocks):
        @pl.loop(0, chans // tile)
        def _(c):
            cols = pl.ds(pl.multiple_of(c * tile, tile), tile)
            taps_c = filt[cols, :]
            hh = dot(fhi[:, :taps], taps_c, NT) + dot(flo[:, :taps], taps_c, NT)
            hr, hi = hh[:taps], hh[taps:]
            for b in blocks:
                x = xbuf[b * taps : (b + 2) * taps, cols]
                xx = dot(fhi[...], x) + dot(flo[...], x)
                xr, xi = xx[:taps], xx[taps:]
                y = jnp.concatenate([xr * hr - xi * hi, xr * hi + xi * hr], 0)
                yh = y.astype(BF)
                yl = (y - yh.astype(F32)).astype(BF)
                res = dot(ghi[...], yh) + dot(ghi[...], yl) + dot(glo[...], yh)
                at = pl.ds(b * taps, taps)
                tbuf[r, at, cols] = (streams[0, at, cols].astype(F32) * res).astype(BF)

    tcopy = remote(tbuf.at[r], tbuf.at[r], t_send, t_recv, {"role": 1 - r})

    def tri():
        return lax.broadcasted_iota(jnp.int32, (toks, toks), 0) >= lax.broadcasted_iota(
            jnp.int32, (toks, toks), 1
        )

    def forward():
        prefix[...] = exc[...].astype(BF)

        @pl.loop(0, heads)
        def _(h):
            q, k, v = qkv[0, :, head(h)], qkv[1, :, head(h)], qkv[2, :, head(h)]
            sc = jnp.where(tri(), dot(q, k, NT), 0.0).astype(BF)
            out[:, head(h)] = scale * (dot(q, prefix[h]) + dot(sc, v))

    whole_rows = rows % LANE == 0

    def add(acc, buf, ctx):
        if not whole_rows:
            return
        at = pl.ds(pl.multiple_of(ctx * rows, LANE), rows)
        acc[...] += dot(tbuf[0, :, at], buf[0, at, :]) + dot(tbuf[1, :, at], buf[1, at, :])

    def add_ring(s):
        add(tcw, wcw, ctx_of(pos - s))
        add(tccw, wccw, ctx_of(pos + s))

    def add_y(s):
        y_in = y_copy(s)
        y_in.wait_recv()
        add(ty, wy, ctx_of(pos + s))

    for acc in (tcw, tccw, ty):
        acc[...] = jnp.zeros_like(acc)
    for copy in local:
        copy.wait()
    for copy in first:
        copy.wait_recv()
    cw_copy(0).start()
    cc_copy(0).start()

    @pl.when(me == 0)
    def _():
        xbuf[pl.ds(0, taps), :] = jnp.zeros((taps, chans), BF)

    mix()

    @pl.when(me + 1 < n)
    def _():
        halo.start()

    own_state()
    scan_send(0, *fwd)
    nblk = toks // taps

    def work1():
        conv(range(1, nblk))

    def work2():
        @pl.when(me >= 1)
        def _():
            halo.wait_recv()

        conv(range(1))
        tcopy.start()

    def work3():
        for k in range(rounds):
            scan_recv(k, *fwd)
            if k + 1 < rounds:
                scan_send(k + 1, *fwd)
        forward()

    def work4():
        tcopy.wait_recv()
        add(tcw, wcw, me)
        add(tccw, wccw, me)
        add(ty, wy, me)
        for s in range(1, 5):
            add_ring(s)
        for s in range(1, 4):
            add_y(s)

    works = {1: work1, 2: work2, 3: work3, 4: work4}
    for s in range(1, 5):
        ring_in(s)
        works[s]()

    @pl.loop(5, n)
    def _(s):
        ring_in(s)
        add_ring(s)
        add_y(s - 1)

    add_y(n - 1)
    if not whole_rows:
        for acc, buf in ((tcw, wcw), (tccw, wccw), (ty, wy)):

            @pl.loop(0, chans // 256)
            def _(c):
                at = pl.ds(pl.multiple_of(c * 256, 256), 256)
                acc[...] += dot(tbuf[0, :, at], buf[0, at, :]) + dot(tbuf[1, :, at], buf[1, at, :])

    def put(at, target):
        resid[:, at] = (tokw[...] * (out[:, at] - target)).astype(BF)

    put(pl.ds(common, cwn), tcw[...])
    put(pl.ds(common + cwn, LANE), tccw[:, :LANE])
    put(pl.ds(pl.multiple_of(g * quarter, LANE), quarter), tccw[:, LANE:])
    put(pl.ds(pl.multiple_of((1 - g) * quarter, LANE), quarter), ty[...])

    exc[...] = jnp.zeros_like(exc)

    @pl.loop(0, heads)
    def _(h):
        own[h] = dot(qkv[0, :, head(h)], resid[:, head(h)], TN)

    scan_send(0, *bwd)

    @pl.loop(0, heads)
    def _(h):
        q, k, v = qkv[0, :, head(h)], qkv[1, :, head(h)], qkv[2, :, head(h)]
        rs = resid[:, head(h)]
        gs = jnp.where(tri(), dot(rs, v, NT), 0.0).astype(BF)
        grads[0, :, head(h)] = (scale * (dot(rs, prefix[h], NT) + dot(gs, k))).astype(BF)
        out[:, head(h)] = dot(gs, q, TN)

    for k in range(rounds):
        scan_recv(k, *bwd)
        if k + 1 < rounds:
            scan_send(k + 1, *bwd)

    @pl.loop(0, heads)
    def _(h):
        q, k, v = qkv[0, :, head(h)], qkv[1, :, head(h)], qkv[2, :, head(h)]
        later = exc[h].astype(BF)
        sc = jnp.where(tri(), dot(q, k, NT), 0.0).astype(BF)
        grads[1, :, head(h)] = (scale * (dot(v, later, NT) + out[:, head(h)])).astype(BF)
        grads[2, :, head(h)] = (scale * (dot(k, later) + dot(sc, resid[:, head(h)], TN))).astype(BF)

    for copy in first:
        copy.wait_send()

    @pl.when(me + 1 < n)
    def _():
        halo.wait_send()

    tcopy.wait_send()
    for k in range(rounds):
        scan_done(k, *fwd)
        scan_done(k, *bwd)

    @pl.loop(0, n - 1)
    def _(s):
        cw_copy(s).wait_send()
        cc_copy(s).wait_send()
        y_copy(s + 1).wait_send()


def on_device(n, teacher_streams, conv_filter, map_weight, bases, base_weights, student_qkv):
    toks, chans = teacher_streams.shape[1:]
    width = student_qkv.shape[2]
    heads = width // DH
    nx = 4 if n % 64 == 0 else 2
    rounds = max(1, (n - 1).bit_length())
    scale = float(DH * toks * n) ** (-0.5)
    onehot = (bases[:, None] == jnp.arange(base_weights.shape[0])[None, :]).astype(F32)
    tokw = jnp.sum(onehot * base_weights[None, :], axis=1, keepdims=True)
    consts = [jnp.asarray(m) for m in transform(conv_filter.shape[1])]
    cwn = width // 2 - LANE
    ccn = width // 4 + LANE
    quarter = width // 4
    dma = pltpu.SemaphoreType.DMA
    state = (rounds, heads, DH, DH)
    scratch = [
        pltpu.VMEM((2, chans, cwn), BF),
        pltpu.VMEM((2, chans, ccn), BF),
        pltpu.VMEM((2, chans, quarter), BF),
        pltpu.VMEM((toks + conv_filter.shape[1], chans), BF),
        pltpu.VMEM((2, toks, chans), BF),
        pltpu.VMEM((toks, cwn), F32),
        pltpu.VMEM((toks, ccn), F32),
        pltpu.VMEM((toks, quarter), F32),
        pltpu.VMEM((toks, width), F32),
        pltpu.VMEM((toks, width), BF),
        pltpu.VMEM((heads, DH, DH), F32),
        pltpu.VMEM((heads, DH, DH), F32),
        pltpu.VMEM((heads, DH, DH), BF),
        pltpu.VMEM(state, BF),
        pltpu.VMEM(state, BF),
        pltpu.VMEM(state, BF),
        pltpu.VMEM(state, BF),
        dma((4,)), dma((4,)), dma((4,)),
        dma((n,)), dma((n,)), dma((n,)), dma((n,)), dma((n,)), dma((n,)),
        dma, dma, dma, dma,
        dma((rounds,)), dma((rounds,)), dma((rounds,)), dma((rounds,)),
    ]
    vmem = pl.BlockSpec(memory_space=pltpu.VMEM)
    return pl.pallas_call(
        functools.partial(kernel, n, nx, scale),
        out_shape=jax.ShapeDtypeStruct((3, toks, width), BF),
        in_specs=[vmem] * 9,
        out_specs=vmem,
        scratch_shapes=scratch,
        compiler_params=pltpu.CompilerParams(
            collective_id=0, has_side_effects=True, vmem_limit_bytes=56 * 1024 * 1024
        ),
    )(teacher_streams, conv_filter, map_weight, tokw, student_qkv, *consts)


def solution(mesh):
    in_specs = (
        P(None, ("grp", "ctx"), "role"),
        P("role", None),
        P(("role", "ctx"), None),
        P(("grp", "ctx")),
        P(),
        P(None, ("grp", "ctx"), "role"),
    )
    out_specs = P(None, ("grp", "ctx"), "role")
    return jax.shard_map(
        functools.partial(on_device, mesh.shape["ctx"]),
        mesh=mesh,
        in_specs=in_specs,
        out_specs=out_specs,
        check_vma=False,
    )
```

time: 350 us -> 163 us (0.47)
  waiting for transfers between devices: 169 us -> 0 us
  Pallas kernels: 0 us -> 157 us
  matrix products: 105 us -> 0 us
  other arithmetic: 30.7 us -> 0.78 us
  local copies, waits for them, and re-layouts: 24.8 us -> 4.72 us
  between operations: 13.5 us -> 0.01 us
  starting transfers between devices: 5.94 us -> 0 us
    all_gather x3 -> x0, waiting for transfers between devices: 159 us -> none  [the longest x2 118 us: prefix(): pieces = lax.all_gather(value, axis)]
    pallas_call x0 -> x1, Pallas kernels: none -> 157 us  [on_device(): pl.pallas_call(functools.partial(kernel, n, nx, scale), out_shape=jax.Sha...]
    conv_general_dilated x1 -> x0, matrix products: 65.3 us -> none  [depthwise(): lax.conv_general_dilated(extended[None], kernel, (1,), 'VALID', dimension...]
    dot_general x13 -> x0, matrix products: 40 us -> none  [the longest x1 11.5 us: on_device(): jnp.dot(columns, shard_rows, preferred_element_type=jnp.float32)]
    select_n x14 -> x0, other arithmetic: 17.2 us -> none  [turn(): return jnp.where(position < mine, longer, so_far)]
    convert_element_type x3 -> x0, other arithmetic: 9.66 us -> none  [the longest x2 6.18 us: on_device(): mixed_in = (teacher_streams[1].astype(jnp.float32) * teacher_streams[2].a...]
    ppermute x1 -> x0, waiting for transfers between devices: 8.95 us -> none  [from_behind(): lax.ppermute(value, axis, [(source, source + steps) for source in range(l...]
    rev x2 -> x0, local copies, waits for them, and re-layouts: 6.09 us -> none  [the longest x1 4.63 us: prefix(): pieces = pieces[::-1]]
  transfers between devices with their start and end apart: 5 -> 0, of which waited for: 4 -> 0; matrix products, arithmetic and copies ran while one was open for 36% -> 0% of each run, Pallas kernels for 0% -> 0%
where the time goes in v1:
time: 163 us
  Pallas kernels  157 us (96%)
  local copies, waits for them, and re-layouts  4.72 us (3%)
    pallas_call x1, Pallas kernels, on_device(): pl.pallas_call(functools.partial(kernel, n, nx, scale), out_shape=jax.Sha...  157 us
    unnamed x1, local copies, waits for them, and re-layouts  3.86 us

profile of v1, /device:TPU:0, one launch (start us, length us, event | category | flops | bytes accessed | tf_op | source)
XLA Modules:
  0.0 162.6 jit_solution(3002956338339638406)
XLA Ops:
  0.0 0.8 select_reduce_fusion
  0.8 0.9 copy.12.tokw
  1.6 157.1 %shard_map.100 = bf16[3,512,1024]{2,1,0:T(8,128)(2,1)} custom-call(bf16[3,512,2048]{2,1,0:T(8,128)(2,1)} %streams.1, bf16[2048,128]{1,0:T(8,128)(2,1)} %filt.1, bf16[256,2048]{1,0:T(8,128)(2,1)} %wmap.1, f32[512,1]{1,0:T(8,128)} %copy.12.tokw, bf16[3,512,1024]{2,1,0:T(8,128)(2,1)} %qkv.1, bf16[256,256]{1,0:T(8,128)(2,1)} %constant.11.clone.fhi, ...), custom_call_target="tpu_custom_call" | custom-call | tf_op jit(solution)/shard_map/pallas_call | solution.py:431
  158.7 3.9 %copy.14 = bf16[3,512,1024]{2,1,0:T(8,128)(2,1)} copy(bf16[3,512,1024]{2,1,0:T(8,128)(2,1)} %shard_map.100) | data formatting | bytes 6291456

commit v2 on v1

--- a/solution.py
+++ b/solution.py
@@ -40,10 +40,10 @@
 
 def kernel(
     n, nx, scale,
-    streams, filt, wmap, tokw, qkv, fhi, flo, ghi, glo,
+    streams_in, filt, wmap, tokw, qkv, fhi, flo, ghi, glo,
     grads,
-    wcw, wccw, wy, xbuf, tbuf, tcw, tccw, ty, out, resid, own, exc, prefix, hsend, hrecv, bsend, brecv,
-    in_loc, in_send, in_recv, cw_send, cw_recv, cc_send, cc_recv, y_send, y_recv,
+    streams, hbuf, wcw, wccw, wy, xbuf, tbuf, tcw, tccw, ty, out, resid, own, exc, prefix, hsend, hrecv, bsend, brecv,
+    st_sem, in_loc, in_send, in_recv, cw_send, cw_recv, cc_send, cc_recv, y_send, y_recv,
     halo_send, halo_recv, t_send, t_recv, h_ssem, h_rsem, b_ssem, b_rsem,
 ):
     toks, chans = streams.shape[1], streams.shape[2]
@@ -114,48 +114,51 @@
     ]
     for copy in first:
         copy.start()
+    fetch = pltpu.make_async_copy(streams_in, streams, st_sem)
+    fetch.start()
     local = [
         pltpu.make_async_copy(src, dst, in_loc.at[i]) for i, (src, dst) in enumerate(shares(r))
     ]
     for copy in local:
         copy.start()
 
-    def cw_copy(s):
-        at = span(ctx_of(pos - s))
-        return remote(wcw.at[:, at, :], wcw.at[:, at, :], cw_send.at[s], cw_recv.at[s], {"ctx": nxt})
-
-    def cw_in(s):
-        at = span(ctx_of(pos - s))
-        return remote(wcw.at[:, at, :], wcw.at[:, at, :], cw_send.at[s - 1], cw_recv.at[s - 1], {"ctx": nxt})
-
-    def cc_copy(s):
-        at = span(ctx_of(pos + s))
-        return remote(wccw.at[:, at, :], wccw.at[:, at, :], cc_send.at[s], cc_recv.at[s], {"ctx": prv})
-
-    def cc_in(s):
-        at = span(ctx_of(pos + s))
-        return remote(wccw.at[:, at, :], wccw.at[:, at, :], cc_send.at[s - 1], cc_recv.at[s - 1], {"ctx": prv})
-
-    def y_copy(s):
+    def move(src, dst, ctx, part, ssem, rsem, s, peer):
+        at = span(ctx)
+        return remote(src.at[part, at, :], dst.at[part, at, :], ssem.at[s, part], rsem.at[s, part], peer)
+
+    def cw_copy(s, part):
+        return move(wcw, wcw, ctx_of(pos - s), part, cw_send, cw_recv, s, {"ctx": nxt})
+
+    def cw_in(s, part):
+        return move(wcw, wcw, ctx_of(pos - s), part, cw_send, cw_recv, s - 1, {"ctx": nxt})
+
+    def cc_copy(s, part):
+        return move(wccw, wccw, ctx_of(pos + s), part, cc_send, cc_recv, s, {"ctx": prv})
+
+    def cc_in(s, part):
+        return move(wccw, wccw, ctx_of(pos + s), part, cc_send, cc_recv, s - 1, {"ctx": prv})
+
+    def y_copy(s, part):
         at = span(ctx_of(pos + s))
         return remote(
-            wccw.at[:, at, pl.ds(LANE, quarter)], wy.at[:, at, :], y_send.at[s], y_recv.at[s], {"grp": 1 - g}
+            wccw.at[part, at, pl.ds(LANE, quarter)],
+            wy.at[part, at, :],
+            y_send.at[s, part],
+            y_recv.at[s, part],
+            {"grp": 1 - g},
         )
 
-    def ring_in(s):
-        cw_in(s).wait_recv()
-        cc_in(s).wait_recv()
-
-        def onward():
-            cw_copy(s).start()
-            cc_copy(s).start()
-
-        if isinstance(s, int):
-            if s < n - 1:
-                onward()
-        else:
-            pl.when(s < n - 1)(onward)
-        y_copy(s).start()
+    def ring_in(s, part):
+        def go(arrived, copy):
+            arrived.wait_recv()
+            if not isinstance(s, int):
+                pl.when(s < n - 1)(lambda: copy(s, part).start())
+            elif s < n - 1:
+                copy(s, part).start()
+
+        go(cw_in(s, part), cw_copy)
+        go(cc_in(s, part), cc_copy)
+        y_copy(s, part).start()
 
     def mix():
         @pl.loop(0, toks // 128)
@@ -211,23 +214,27 @@
 
     tile = 256
 
-    def conv(blocks):
+    def filters():
         @pl.loop(0, chans // tile)
         def _(c):
             cols = pl.ds(pl.multiple_of(c * tile, tile), tile)
             taps_c = filt[cols, :]
-            hh = dot(fhi[:, :taps], taps_c, NT) + dot(flo[:, :taps], taps_c, NT)
-            hr, hi = hh[:taps], hh[taps:]
-            for b in blocks:
-                x = xbuf[b * taps : (b + 2) * taps, cols]
-                xx = dot(fhi[...], x) + dot(flo[...], x)
-                xr, xi = xx[:taps], xx[taps:]
-                y = jnp.concatenate([xr * hr - xi * hi, xr * hi + xi * hr], 0)
-                yh = y.astype(BF)
-                yl = (y - yh.astype(F32)).astype(BF)
-                res = dot(ghi[...], yh) + dot(ghi[...], yl) + dot(glo[...], yh)
-                at = pl.ds(b * taps, taps)
-                tbuf[r, at, cols] = (streams[0, at, cols].astype(F32) * res).astype(BF)
+            hbuf[:, cols] = dot(fhi[:, :taps], taps_c, NT) + dot(flo[:, :taps], taps_c, NT)
+
+    def conv(b):
+        @pl.loop(0, chans // tile)
+        def _(c):
+            cols = pl.ds(pl.multiple_of(c * tile, tile), tile)
+            hr, hi = hbuf[:taps, cols], hbuf[taps:, cols]
+            x = xbuf[b * taps : (b + 2) * taps, cols]
+            xx = dot(fhi[...], x) + dot(flo[...], x)
+            xr, xi = xx[:taps], xx[taps:]
+            y = jnp.concatenate([xr * hr - xi * hi, xr * hi + xi * hr], 0)
+            yh = y.astype(BF)
+            yl = (y - yh.astype(F32)).astype(BF)
+            res = dot(ghi[...], yh) + dot(ghi[...], yl) + dot(glo[...], yh)
+            at = pl.ds(b * taps, taps)
+            tbuf[r, at, cols] = (streams[0, at, cols].astype(F32) * res).astype(BF)
 
     tcopy = remote(tbuf.at[r], tbuf.at[r], t_send, t_recv, {"role": 1 - r})
 
@@ -236,14 +243,19 @@
             jnp.int32, (toks, toks), 1
         )
 
-    def forward():
-        prefix[...] = exc[...].astype(BF)
-
-        @pl.loop(0, heads)
+    def inside(low, high):
+        @pl.loop(low, high)
         def _(h):
             q, k, v = qkv[0, :, head(h)], qkv[1, :, head(h)], qkv[2, :, head(h)]
             sc = jnp.where(tri(), dot(q, k, NT), 0.0).astype(BF)
-            out[:, head(h)] = scale * (dot(q, prefix[h]) + dot(sc, v))
+            out[:, head(h)] = dot(sc, v)
+
+    def outside():
+        prefix[...] = exc[...].astype(BF)
+
+        @pl.loop(0, heads)
+        def _(h):
+            out[:, head(h)] = scale * (dot(qkv[0, :, head(h)], prefix[h]) + out[:, head(h)])
 
     whole_rows = rows % LANE == 0
 
@@ -258,23 +270,23 @@
         add(tccw, wccw, ctx_of(pos + s))
 
     def add_y(s):
-        y_in = y_copy(s)
-        y_in.wait_recv()
+        for part in range(2):
+            y_copy(s, part).wait_recv()
         add(ty, wy, ctx_of(pos + s))
 
-    for acc in (tcw, tccw, ty):
-        acc[...] = jnp.zeros_like(acc)
     for copy in local:
         copy.wait()
     for copy in first:
         copy.wait_recv()
-    cw_copy(0).start()
-    cc_copy(0).start()
+    for part in range(2):
+        cw_copy(0, part).start()
+        cc_copy(0, part).start()
 
     @pl.when(me == 0)
     def _():
         xbuf[pl.ds(0, taps), :] = jnp.zeros((taps, chans), BF)
 
+    fetch.wait()
     mix()
 
     @pl.when(me + 1 < n)
@@ -283,44 +295,58 @@
 
     own_state()
     scan_send(0, *fwd)
+    filters()
+    for acc in (tcw, tccw, ty):
+        acc[...] = jnp.zeros_like(acc)
     nblk = toks // taps
 
-    def work1():
-        conv(range(1, nblk))
-
-    def work2():
+    def halo_in():
         @pl.when(me >= 1)
         def _():
             halo.wait_recv()
 
-        conv(range(1))
-        tcopy.start()
-
-    def work3():
-        for k in range(rounds):
+    def scan_step(k):
+        if k < rounds:
             scan_recv(k, *fwd)
             if k + 1 < rounds:
                 scan_send(k + 1, *fwd)
-        forward()
-
-    def work4():
+
+    def own_share():
         tcopy.wait_recv()
         add(tcw, wcw, me)
         add(tccw, wccw, me)
         add(ty, wy, me)
-        for s in range(1, 5):
-            add_ring(s)
-        for s in range(1, 4):
-            add_y(s)
-
-    works = {1: work1, 2: work2, 3: work3, 4: work4}
-    for s in range(1, 5):
-        ring_in(s)
-        works[s]()
-
-    @pl.loop(5, n)
+
+    def last_scans():
+        for k in range(4, rounds):
+            scan_step(k)
+
+    works = {
+        (1, 0): [lambda: conv(1)],
+        (1, 1): [lambda: conv(2)],
+        (2, 0): [lambda: [conv(b) for b in range(3, nblk)]],
+        (2, 1): [halo_in, lambda: conv(0), tcopy.start],
+        (3, 0): [lambda: scan_step(0), lambda: inside(0, heads // 2)],
+        (3, 1): [lambda: inside(heads // 2, heads)],
+        (4, 0): [lambda: scan_step(1), own_share],
+        (4, 1): [lambda: add_ring(1)],
+        (5, 0): [lambda: scan_step(2), lambda: add_ring(2), lambda: add_y(1)],
+        (5, 1): [lambda: add_ring(3), lambda: add_y(2)],
+        (6, 0): [lambda: scan_step(3), lambda: add_ring(4), lambda: add_y(3)],
+        (6, 1): [lambda: add_ring(5), lambda: add_y(4)],
+        (7, 0): [last_scans, outside, lambda: add_ring(6), lambda: add_y(5)],
+        (7, 1): [lambda: add_y(6), lambda: add_ring(7)],
+    }
+    for s in range(1, 8):
+        for part in range(2):
+            ring_in(s, part)
+            for work in works[s, part]:
+                work()
+
+    @pl.loop(8, n)
     def _(s):
-        ring_in(s)
+        for part in range(2):
+            ring_in(s, part)
         add_ring(s)
         add_y(s - 1)
 
@@ -384,9 +410,10 @@
 
     @pl.loop(0, n - 1)
     def _(s):
-        cw_copy(s).wait_send()
-        cc_copy(s).wait_send()
-        y_copy(s + 1).wait_send()
+        for part in range(2):
+            cw_copy(s, part).wait_send()
+            cc_copy(s, part).wait_send()
+            y_copy(s + 1, part).wait_send()
 
 
 def on_device(n, teacher_streams, conv_filter, map_weight, bases, base_weights, student_qkv):
@@ -405,6 +432,8 @@
     dma = pltpu.SemaphoreType.DMA
     state = (rounds, heads, DH, DH)
     scratch = [
+        pltpu.VMEM(teacher_streams.shape, BF),
+        pltpu.VMEM((2 * conv_filter.shape[1], chans), F32),
         pltpu.VMEM((2, chans, cwn), BF),
         pltpu.VMEM((2, chans, ccn), BF),
         pltpu.VMEM((2, chans, quarter), BF),
@@ -422,8 +451,8 @@
         pltpu.VMEM(state, BF),
         pltpu.VMEM(state, BF),
         pltpu.VMEM(state, BF),
-        dma((4,)), dma((4,)), dma((4,)),
-        dma((n,)), dma((n,)), dma((n,)), dma((n,)), dma((n,)), dma((n,)),
+        dma, dma((4,)), dma((4,)), dma((4,)),
+        dma((n, 2)), dma((n, 2)), dma((n, 2)), dma((n, 2)), dma((n, 2)), dma((n, 2)),
         dma, dma, dma, dma,
         dma((rounds,)), dma((rounds,)), dma((rounds,)), dma((rounds,)),
     ]
@@ -431,7 +460,7 @@
     return pl.pallas_call(
         functools.partial(kernel, n, nx, scale),
         out_shape=jax.ShapeDtypeStruct((3, toks, width), BF),
-        in_specs=[vmem] * 9,
+        in_specs=[pl.BlockSpec(memory_space=pl.ANY)] + [vmem] * 8,
         out_specs=vmem,
         scratch_shapes=scratch,
         compiler_params=pltpu.CompilerParams(

time: 163 us -> 152 us (0.933)
  Pallas kernels: 157 us -> 146 us
    pallas_call x1, Pallas kernels: 157 us -> 146 us  [on_device(): pl.pallas_call(functools.partial(kernel, n, nx, scale), out_shape=jax.Sha...]
where the time goes in v2:
time: 152 us; the launch traced here: 151 us
  Pallas kernels  146 us (96%)
  local copies, waits for them, and re-layouts  4.72 us (3%)
    pallas_call x1, Pallas kernels, on_device(): pl.pallas_call(functools.partial(kernel, n, nx, scale), out_shape=jax.Sha...  146 us
    unnamed x1, local copies, waits for them, and re-layouts  3.86 us

profile of v2, /device:TPU:0, one launch (start us, length us, event | category | flops | bytes accessed | tf_op | source)
XLA Modules:
  0.0 151.3 jit_solution(12409256974003945324)
XLA Ops:
  0.0 0.8 select_reduce_fusion
  0.8 0.9 copy.12.tokw
  1.6 145.8 %shard_map.100 = bf16[3,512,1024]{2,1,0:T(8,128)(2,1)} custom-call(bf16[3,512,2048]{2,1,0:T(8,128)(2,1)} %streams_in.1, bf16[2048,128]{1,0:T(8,128)(2,1)} %filt.1, bf16[256,2048]{1,0:T(8,128)(2,1)} %wmap.1, f32[512,1]{1,0:T(8,128)} %copy.12.tokw, bf16[3,512,1024]{2,1,0:T(8,128)(2,1)} %qkv.1, bf16[256,256]{1,0:T(8,128)(2,1)} %constant.11.clone.fhi, ...), custom_call_target="tpu_custom_call" | custom-call | tf_op jit(solution)/shard_map/pallas_call | solution.py:460
  147.5 3.9 %copy.14 = bf16[3,512,1024]{2,1,0:T(8,128)(2,1)} copy(bf16[3,512,1024]{2,1,0:T(8,128)(2,1)} %shard_map.100) | data formatting | bytes 6291456

commit v3 on v2

--- a/solution.py
+++ b/solution.py
@@ -318,7 +318,7 @@
         add(ty, wy, me)
 
     def last_scans():
-        for k in range(4, rounds):
+        for k in range(2, rounds):
             scan_step(k)
 
     works = {
@@ -326,16 +326,16 @@
         (1, 1): [lambda: conv(2)],
         (2, 0): [lambda: [conv(b) for b in range(3, nblk)]],
         (2, 1): [halo_in, lambda: conv(0), tcopy.start],
-        (3, 0): [lambda: scan_step(0), lambda: inside(0, heads // 2)],
-        (3, 1): [lambda: inside(heads // 2, heads)],
-        (4, 0): [lambda: scan_step(1), own_share],
+        (3, 0): [lambda: inside(0, heads // 2)],
+        (3, 1): [lambda: scan_step(0), lambda: inside(heads // 2, heads)],
+        (4, 0): [own_share],
         (4, 1): [lambda: add_ring(1)],
-        (5, 0): [lambda: scan_step(2), lambda: add_ring(2), lambda: add_y(1)],
+        (5, 0): [lambda: scan_step(1), lambda: add_ring(2), lambda: add_y(1)],
         (5, 1): [lambda: add_ring(3), lambda: add_y(2)],
-        (6, 0): [lambda: scan_step(3), lambda: add_ring(4), lambda: add_y(3)],
+        (6, 0): [lambda: add_ring(4), lambda: add_y(3)],
         (6, 1): [lambda: add_ring(5), lambda: add_y(4)],
-        (7, 0): [last_scans, outside, lambda: add_ring(6), lambda: add_y(5)],
-        (7, 1): [lambda: add_y(6), lambda: add_ring(7)],
+        (7, 0): [lambda: add_ring(6), lambda: add_y(5)],
+        (7, 1): [last_scans, outside, lambda: add_y(6), lambda: add_ring(7)],
     }
     for s in range(1, 8):
         for part in range(2):

time: 152 us -> 152 us (level)
  no operation moved by 1% of the time
where the time goes in v3:
time: 152 us; the launch traced here: 151 us
  Pallas kernels  146 us (96%)
  local copies, waits for them, and re-layouts  4.72 us (3%)
    pallas_call x1, Pallas kernels, on_device(): pl.pallas_call(functools.partial(kernel, n, nx, scale), out_shape=jax.Sha...  146 us
    unnamed x1, local copies, waits for them, and re-layouts  3.86 us

profile of v3, /device:TPU:0, one launch (start us, length us, event | category | flops | bytes accessed | tf_op | source)
XLA Modules:
  0.0 151.3 jit_solution(4558061952268418647)
XLA Ops:
  0.0 0.8 select_reduce_fusion
  0.8 0.9 copy.12.tokw
  1.6 145.8 %shard_map.100 = bf16[3,512,1024]{2,1,0:T(8,128)(2,1)} custom-call(bf16[3,512,2048]{2,1,0:T(8,128)(2,1)} %streams_in.1, bf16[2048,128]{1,0:T(8,128)(2,1)} %filt.1, bf16[256,2048]{1,0:T(8,128)(2,1)} %wmap.1, f32[512,1]{1,0:T(8,128)} %copy.12.tokw, bf16[3,512,1024]{2,1,0:T(8,128)(2,1)} %qkv.1, bf16[256,256]{1,0:T(8,128)(2,1)} %constant.11.clone.fhi, ...), custom_call_target="tpu_custom_call" | custom-call | tf_op jit(solution)/shard_map/pallas_call | solution.py:460
  147.5 3.9 %copy.14 = bf16[3,512,1024]{2,1,0:T(8,128)(2,1)} copy(bf16[3,512,1024]{2,1,0:T(8,128)(2,1)} %shard_map.100) | data formatting | bytes 6291456
